TPU v7x, 256 devices: a whole 4x4x8 slice. The times are simulated.
256 devices in a mesh: dp: 16 (over y, z_hi, core), seq: 16 (over x, z_lo).
Axes of the slice: x: 4, y: 4, z: 8 (z_hi: 2, z_lo: 4; z = z_hi * 4 + z_lo), core: 2. Of those that a mesh axis runs over, the one named last changes fastest.
Arguments:
- queries: bfloat16 [16, 2048, 4096], P('dp', 'seq'), may hold values from -8 to 8
- key_vectors: bfloat16 [16, 2048, 4096], P('dp', 'seq'), may hold values from -8 to 8
- value_vectors: bfloat16 [16, 2048, 4096], P('dp', 'seq'), may hold values from -6 to 6
- cotangent: bfloat16 [16, 2048, 4096], P('dp', 'seq'), may hold values from -6 to 6
- conv_weight: float32 [32, 9], P('seq'), may hold values from -1 to 1
Outputs:
- query_grad: bfloat16 [16, 2048, 4096], P('dp', 'seq')
- key_grad: bfloat16 [16, 2048, 4096], P('dp', 'seq')
- value_grad: bfloat16 [16, 2048, 4096], P('dp', 'seq')
- conv_grad: float32 [32, 9], P('seq')
All inputs are finite; a program needn't handle non-finite values.
Results may differ from a plain program's by a relative error of at most 0.018.
The roundings to bfloat16 on the way count: a program that leaves them out, or rounds other values in their place, can miss the bound.
Values may be sent and summed in bfloat16 or wider, within the bound.
A program may use at most 128 MiB of HBM per device.

v0:
```python
import jax
import jax.numpy as jnp
from jax import lax
from jax.experimental import pallas as pl
from jax.experimental.pallas import tpu as pltpu
from jax.sharding import PartitionSpec as P

HD = 128
LM = 128
ITERS = 6
KW = 9
SEG = 16
SCALE = HD ** (-0.5)
MESH = pl.DeviceIdType.MESH
BF = jnp.bfloat16
F32 = jnp.float32

NST = 2
RUNS = 4
RUN = 256
EXT = RUN + 32
ORDER = (1, 0, 3, 2)


def dot(a, b, ca=1, cb=0):
    return lax.dot_general(a, b, (((ca,), (cb,)), ((), ())), preferred_element_type=F32)


def split(x):
    high = x.astype(BF)
    return high, (x - high.astype(F32)).astype(BF)


def mm3(a, b):
    left = jnp.concatenate([a[0], a[1], a[0]], axis=1)
    right = jnp.concatenate([b[0], b[0], b[1]], axis=0)
    return dot(left, right)


def rounded(x):
    return x.astype(BF).astype(F32)


def kernel(
    q_in, k_in, v_in, g_in, w_in,
    dq_out, dk_out, dv_out, dw_out,
    qk_full, lm_local, lm_all, marks, w_all, taps_mat,
    land, halo, rf, rt, lf, stats, part, part_in, mxds, delta,
    m_save, inv_save, xt_save, p_save, p2_save, j_save, al_save,
    dkq, dkq_in, mid_grad, tg, dq_buf, out_buf, dw_buf, dw_dp,
    s_loc, s_lm, r_lm, s_lmf, r_lmf, s_in, r_in, s_own, s_w, r_w, s_ms, r_ms,
    s_part, r_part, s_halo, r_halo, s_mx, r_mx, s_dl, r_dl, s_dkq, r_dkq, s_tg, r_tg,
    s_out, r_out, s_outl, s_dw, r_dw, s_dp, r_dp,
):
    dp = lax.axis_index("dp")
    seq = lax.axis_index("seq")
    x = seq // 4
    z = seq % 4
    za = z // 2
    zb = z % 2
    other = 1 - za
    group = x * 2 + zb
    ins = (q_in, k_in, v_in, g_in)
    outs = (dq_out, dk_out, dv_out)
    pending = []

    def member(i):
        p = (group + i) % 8
        return p, (p // 2) * 4 + za * 2 + p % 2

    partner = x * 4 + other * 2 + zb
    cross = x * 4 + other * 2 + (1 - zb)

    def dp_peer(b):
        step = 1 << b
        return dp + step - 2 * step * ((dp // step) % 2)

    def remote(src, dst, ss, rs, to, at=None):
        copy = pltpu.make_async_remote_copy(
            src_ref=src, dst_ref=dst, send_sem=ss, recv_sem=rs,
            device_id=(dp if at is None else at, to), device_id_type=MESH,
        )
        copy.start()
        pending.append(copy)
        return copy

    local = []
    for n, ref in enumerate((q_in, k_in)):
        copy = pltpu.make_async_copy(ref.at[0], qk_full.at[n], s_loc.at[n])
        copy.start()
        local.append(copy)
    halo[...] = jnp.zeros_like(halo)
    w_all[...] = jnp.zeros_like(w_all)
    w_all[z, 0:2, 0:KW] = w_in[...]
    barrier = pltpu.get_barrier_semaphore()
    for i in range(1, 8):
        pl.semaphore_signal(barrier, inc=1, device_id=(dp, member(i)[1]), device_id_type=MESH)
    for to in (partner, cross):
        pl.semaphore_signal(barrier, inc=1, device_id=(dp, to), device_id_type=MESH)
    for b in range(4):
        pl.semaphore_signal(barrier, inc=1, device_id=(dp_peer(b), seq), device_id_type=MESH)
    for copy in local:
        copy.wait()
    rows = lax.broadcasted_iota(jnp.int32, (8, 128), 0)
    cols = lax.broadcasted_iota(jnp.int32, (8, 128), 1)
    averager = jnp.where(cols // SEG == rows, 1.0 / SEG, 0.0).astype(BF)
    for c in range(8):
        cut = slice(512 * c, 512 * c + 512)
        lm_local[:, cut] = jnp.concatenate(
            [dot(averager, qk_full[0, :, cut]), dot(averager, qk_full[1, :, cut])], axis=0
        ).astype(BF)
    pl.semaphore_wait(barrier, 13)

    my_cols = pl.ds(pl.multiple_of(group * 512, 512), 512)
    lm_copies = []
    for i in range(1, 8):
        p, to = member(i)
        lm_copies.append(remote(
            lm_local.at[:, pl.ds(pl.multiple_of(p * 512, 512), 512)], lm_all.at[za, group],
            s_lm.at[i - 1], r_lm.at[i - 1], to))
    lm_own = pltpu.make_async_copy(lm_local.at[:, my_cols], lm_all.at[za, group], s_loc.at[2])
    lm_own.start()
    w_copies = [
        remote(w_all.at[z], w_all.at[z], s_w.at[n], r_w.at[n], to)
        for n, to in enumerate((x * 4 + za * 2 + 1 - zb, partner, cross))
    ]
    in_copies = {}
    for st in range(NST):
        for a in ORDER:
            got = []
            spot = land.at[a, st, x, pl.ds(pl.multiple_of(zb * 128, 128), 128)]
            for i in range(1, 8):
                p, to = member(i)
                cut = pl.ds(pl.multiple_of(p * 512 + st * 256, 256), 256)
                got.append(remote(
                    ins[a].at[0, :, cut], spot, s_in.at[st, a, i - 1], r_in.at[st, a, i - 1], to))
            cut = pl.ds(pl.multiple_of(group * 512 + st * 256, 256), 256)
            own = pltpu.make_async_copy(ins[a].at[0, :, cut], spot, s_own.at[st, a])
            own.start()
            in_copies[st, a] = (got, own)

    def arrive(st, a):
        got, own = in_copies[st, a]
        for copy in got:
            copy.wait_recv()
        own.wait()

    for copy in lm_copies:
        copy.wait_recv()
    lm_own.wait()
    lmf = remote(lm_all.at[za], lm_all.at[za], s_lmf, r_lmf, partner)
    for copy in w_copies:
        copy.wait_recv()

    t_at = lax.broadcasted_iota(jnp.int32, (RUN, EXT), 0)
    u_at = lax.broadcasted_iota(jnp.int32, (RUN, EXT), 1)
    for h in range(4):
        taps = w_all[2 * zb + h // 2, h % 2 : h % 2 + 1, :]
        band = jnp.zeros((RUN, EXT), F32)
        for j in range(KW):
            band = jnp.where(t_at + 20 - u_at == j, taps[:, j : j + 1], band)
        high, low = split(band)
        taps_mat[h, 0] = high
        taps_mat[h, 1] = low

    lmf.wait_recv()
    lm_values = lm_all[...].astype(F32)
    for h in range(4):
        piece = lm_values[:, :, :, 128 * h : 128 * h + 128]
        marks[0, h] = piece[:, :, 0:8].reshape(LM, HD).astype(BF)
        marks[1, h] = piece[:, :, 8:16].reshape(LM, HD).astype(BF)

    r_at = lax.broadcasted_iota(jnp.int32, (LM, LM), 0)
    c_at = lax.broadcasted_iota(jnp.int32, (LM, LM), 1)
    eye = jnp.where(r_at == c_at, 1.0, 0.0).astype(F32)
    state = []
    for st in range(NST):
        logits = dot(marks[0, 2 * st + za], marks[1, 2 * st + za], 1, 1) * SCALE
        e = jnp.exp(logits - jnp.max(logits, axis=1, keepdims=True))
        middle = e / jnp.sum(e, axis=1, keepdims=True)
        top = jnp.max(jnp.sum(middle, axis=0, keepdims=True), axis=1, keepdims=True)
        side = jnp.max(jnp.sum(middle, axis=1, keepdims=True), axis=0, keepdims=True)
        al = 1.0 / (top * side)
        m_save[st] = middle
        al_save[st] = jnp.broadcast_to(al, (8, 128))
        x0 = al * middle.T
        state.append([x0, mm3(split(middle), split(x0))])
    for it in range(ITERS):
        for st in range(NST):
            inv, prod = state[st]
            ps = split(prod)
            prod2 = mm3(ps, ps)
            p2s = split(prod2)
            j_mat = 13.0 * eye - 15.0 * prod + mm3(p2s, split(7.0 * eye - prod))
            js = split(j_mat)
            xts = split(inv.T)
            for n in range(2):
                xt_save[st, it, n] = xts[n]
                p_save[st, it, n] = ps[n]
                p2_save[st, it, n] = p2s[n]
                j_save[st, it, n] = js[n]
            new = 0.25 * mm3(split(inv), js)
            if it < ITERS - 1:
                prod = 0.25 * (13.0 * prod - 15.0 * prod2 + mm3(p2s, split(7.0 * prod - prod2)))
            state[st] = [new, prod]
    for st in range(NST):
        inv_save[st] = state[st][0]

    dw_state = {}

    def dw_start():
        dw_buf[z] = dw_buf[4]
        dw_state["z"] = [
            remote(dw_buf.at[4], dw_buf.at[z], s_dw.at[n], r_dw.at[n], to)
            for n, to in enumerate((x * 4 + za * 2 + 1 - zb, partner, cross))
        ]

    def dw_step(b):
        if b == 0:
            for copy in dw_state["z"]:
                copy.wait_recv()
            both = dw_buf[z // 2] + dw_buf[z // 2 + 2]
            dw_dp[0] = jnp.where(z % 2 == 0, both, jnp.concatenate([both[2:8], both[0:2]], axis=0))
        else:
            dw_state["dp"].wait_recv()
            dw_dp[2 * b] = dw_dp[2 * b - 2] + dw_dp[2 * b - 1]
        if b < 4:
            dw_state["dp"] = remote(
                dw_dp.at[2 * b], dw_dp.at[2 * b + 1], s_dp.at[b], r_dp.at[b], seq, at=dp_peer(b))
        else:
            dw_out[...] = dw_dp[8, 0:2, 0:KW]

    dw_buf[4] = jnp.zeros((8, 128), F32)
    lane = lax.broadcasted_iota(jnp.int32, (1, 128), 1)

    for st in range(NST):

        def head(a, j):
            return land[a, st, :, :, 128 * j : 128 * j + 128].reshape(RUNS * RUN, HD)

        last = st == NST - 1
        arrive(st, 1)
        for j in range(2):
            logits = dot(head(1, j), marks[0, 2 * st + j], 1, 1) * SCALE
            m = jnp.max(logits, axis=0, keepdims=True)
            e = jnp.exp(logits - m)
            rf[st, j] = e
            stats[st, za, 2 * j : 2 * j + 1, :] = m
            stats[st, za, 2 * j + 1 : 2 * j + 2, :] = jnp.sum(e, axis=0, keepdims=True)
        ms = remote(stats.at[st, za], stats.at[st, za], s_ms.at[st], r_ms.at[st], partner)
        arrive(st, 0)
        for j in range(2):
            logits = dot(marks[1, 2 * st + j], head(0, j), 1, 1) * SCALE
            e = jnp.exp(logits - jnp.max(logits, axis=0, keepdims=True))
            lf[st, j] = e * (1.0 / jnp.sum(e, axis=0, keepdims=True))
        ms.wait_recv()
        for j in range(2):
            m1 = stats[st, za, 2 * j : 2 * j + 1, :]
            s1 = stats[st, za, 2 * j + 1 : 2 * j + 2, :]
            m2 = stats[st, other, 2 * j : 2 * j + 1, :]
            s2 = stats[st, other, 2 * j + 1 : 2 * j + 2, :]
            m = jnp.maximum(m1, m2)
            e1 = jnp.exp(m1 - m)
            factor = e1 / (s1 * e1 + s2 * jnp.exp(m2 - m))
            value = rf[st, j] * factor
            rf[st, j] = value
            rt[st, j] = value.astype(BF)
        arrive(st, 3)
        for j in range(2):
            part[st, j, 0] = dot(lf[st, j].astype(BF), head(3, j))
        dm_copy = remote(
            part.at[st, other, 0], part_in.at[st, 0], s_part.at[st, 0], r_part.at[st, 0], partner)

        def send_halo(a, n):
            return [
                remote(
                    land.at[a, st, :, pl.ds(start, 16)], halo.at[st, n, side, pl.ds(za, 4)],
                    s_halo.at[st, n, side], r_halo.at[st, n, side], partner)
                for side, start in ((0, RUN - 16), (1, 0))
            ]

        halos = send_halo(3, 0)
        arrive(st, 2)
        for j in range(2):
            part[st, j, 1] = dot(rt[st, j], head(2, j), 0, 0)
        sum_copy = remote(
            part.at[st, other, 1], part_in.at[st, 1], s_part.at[st, 1], r_part.at[st, 1], partner)
        halos += send_halo(2, 1)

        def extended(a, n, r, j):
            cut = slice(128 * j, 128 * j + 128)
            return jnp.concatenate(
                [halo[st, n, 0, r, :, cut], land[a, st, r, :, cut], halo[st, n, 1, r + 1, :, cut]],
                axis=0)

        for copy in halos[:2]:
            copy.wait_recv()
        for j in range(2):
            for r in range(RUNS):
                g_ext = extended(3, 0, r, j)
                conv = dot(taps_mat[2 * st + j, 0], g_ext) + dot(taps_mat[2 * st + j, 1], g_ext)
                out_buf[2, st, r, :, 128 * j : 128 * j + 128] = conv.astype(BF)

        dm_copy.wait_recv()
        sum_copy.wait_recv()
        dmix = rounded(part[st, za, 0] + part_in[st, 0])
        summary = part[st, za, 1] + part_in[st, 1]
        inv = inv_save[st]
        dms = dmix.astype(BF)
        mixed = jnp.dot(inv, summary, precision=lax.Precision.HIGHEST, preferred_element_type=F32)
        inv_t = split(inv.T)
        dsum = dot(jnp.concatenate([inv_t[0], inv_t[1]], axis=1),
                   jnp.concatenate([dms, dms], axis=0))
        mxds[st, za, 0] = mixed.astype(BF)
        mxds[st, za, 1] = dsum.astype(BF)
        row = jnp.sum((dsum * summary).T, axis=0, keepdims=True)
        delta[st, za] = jnp.broadcast_to(row, (8, 128))
        mx_copy = remote(mxds.at[st, za], mxds.at[st, za], s_mx.at[st], r_mx.at[st], partner)
        dl_copy = remote(delta.at[st, za], delta.at[st, za], s_dl.at[st], r_dl.at[st], partner)

        for copy in halos[2:]:
            copy.wait_recv()
        for j in range(2):
            corr = jnp.zeros((RUN, EXT), F32)
            for r in range(RUNS):
                cut = slice(128 * j, 128 * j + 128)
                corr += dot(land[3, st, r, :, cut], extended(2, 1, r, j), 1, 1)
            line = jnp.zeros((1, 128), F32)
            for t in range(KW):
                band = jnp.where(u_at - t_at - 12 == t, corr, 0.0)
                total = jnp.sum(jnp.sum(band, axis=0, keepdims=True), axis=1, keepdims=True)
                line = jnp.where(lane == t, total, line)
            dw_buf[4, 2 * st + j : 2 * st + j + 1, :] = line
        if last:
            dw_start()

        s_t = split(summary.T)
        grad = dot(jnp.concatenate([dms, dms], axis=1), jnp.concatenate([s_t[0], s_t[1]], axis=0))
        middle = m_save[st]
        m_t = split(middle.T)
        d_mid = jnp.zeros((LM, LM), F32)
        for it in reversed(range(ITERS)):
            xt = (xt_save[st, it, 0], xt_save[st, it, 1])
            ps = (p_save[st, it, 0], p_save[st, it, 1])
            p2s = (p2_save[st, it, 0], p2_save[st, it, 1])
            js = (j_save[st, it, 0], j_save[st, it, 1])
            ws = split(grad)
            g_mat = 0.25 * mm3(xt, ws)
            gs = split(g_mat)
            u_mat = 7.0 * g_mat - mm3(gs, ps)
            us = split(u_mat)
            d_p = mm3(us, ps) + mm3(ps, us) - mm3(p2s, gs) - 15.0 * g_mat
            dps = split(d_p)
            d_mid = d_mid + mm3(dps, xt)
            grad = 0.25 * mm3(ws, js) + mm3(m_t, dps)
        d_mid = d_mid + al_save[st, 0:1, :] * grad.T
        d_log = middle * (d_mid - jnp.sum(middle * d_mid, axis=1, keepdims=True)) * SCALE
        d_log = d_log.astype(BF)
        mid_grad[0] = dot(d_log, marks[1, 2 * st + za])
        mid_grad[1] = dot(d_log, marks[0, 2 * st + za], 0, 0)
        if last:
            dw_step(0)

        mx_copy.wait_recv()
        dl_copy.wait_recv()
        for j in range(2):
            mixed = mxds[st, j, 0]
            ds = mxds[st, j, 1]
            q_marks, k_marks = marks[0, 2 * st + j], marks[1, 2 * st + j]
            left = lf[st, j]
            d_left = rounded(dot(mixed, head(3, j), 1, 1))
            prod = left * d_left
            d_left = ((prod - left * jnp.sum(prod, axis=0, keepdims=True)) * SCALE).astype(BF)
            d_right = rounded(dot(head(2, j), ds, 1, 1))
            d_right = (rf[st, j] * (d_right - delta[st, j, 0:1, :]) * SCALE).astype(BF)
            dkq[st, j, 0] = dot(d_right, head(1, j), 0, 0).astype(BF)
            dkq[st, j, 1] = dot(d_left, head(0, j)).astype(BF)
            dq_buf[0, j] = dot(d_left, k_marks, 0, 0).astype(BF)
            dq_buf[1, j] = dot(d_right, q_marks).astype(BF)
        dkq_copy = remote(
            dkq.at[st, other], dkq_in.at[st], s_dkq.at[st], r_dkq.at[st], partner)
        for j in range(2):
            cut = slice(128 * j, 128 * j + 128)
            d_v = rounded(dot(rt[st, j], mxds[st, j, 1])).reshape(RUNS, RUN, HD)
            out_buf[2, st, :, :, cut] = (out_buf[2, st, :, :, cut].astype(F32) + d_v).astype(BF)

        def send_out(a):
            spot = outs[a].at[0, :, pl.ds(pl.multiple_of(group * 512 + st * 256, 256), 256)]
            for i in range(1, 8):
                p, to = member(i)
                remote(
                    out_buf.at[a, st, p // 2, pl.ds(pl.multiple_of((p % 2) * 128, 128), 128)], spot,
                    s_out.at[st, a, i - 1], r_out.at[st, a, i - 1], to)
            copy = pltpu.make_async_copy(
                out_buf.at[a, st, x, pl.ds(pl.multiple_of(zb * 128, 128), 128)], spot,
                s_outl.at[st, a])
            copy.start()
            return copy

        own_out = [send_out(2)]
        if last:
            dw_step(1)
        dkq_copy.wait_recv()
        for n in range(2):
            total = rounded(dkq[st, za, n].astype(F32) + dkq_in[st, n].astype(F32))
            total = rounded(total + rounded(mid_grad[n])) * (1.0 / SEG)
            tg[st, za, n] = total.astype(BF).reshape(2, LM // 2, HD)
        tg_copy = remote(
            tg.at[st, za, :, other], tg.at[st, za, :, other], s_tg.at[st], r_tg.at[st], partner)
        if last:
            dw_step(2)
        tg_copy.wait_recv()
        for n in (1, 0):
            for j in range(2):
                rest = tg[st, j, n, za].astype(F32)
                rest = jnp.broadcast_to(rest[:, None, :], (LM // 2, SEG, HD))
                total = dq_buf[n, j].astype(F32) + rest.reshape(RUNS * RUN, HD)
                out_buf[n, st, :, :, 128 * j : 128 * j + 128] = total.astype(BF).reshape(
                    RUNS, RUN, HD)
            own_out.append(send_out(n))
        pending.extend(own_out)

    dw_step(3)
    dw_step(4)
    for copy in pending:
        if copy.is_remote:
            copy.wait_send()
        else:
            copy.wait()
    for st in range(NST):
        for a in range(3):
            for i in range(7):
                spot = outs[a].at[0, :, pl.ds(0, 256)]
                pltpu.make_async_remote_copy(
                    src_ref=spot, dst_ref=spot, send_sem=s_out.at[st, a, i],
                    recv_sem=r_out.at[st, a, i], device_id=(dp, partner), device_id_type=MESH,
                ).wait_recv()


def shards(queries, key_vectors, value_vectors, cotangent, conv_weight):
    any_spec = pl.BlockSpec(memory_space=pl.ANY)
    vmem_spec = pl.BlockSpec(memory_space=pltpu.VMEM)
    full = jax.ShapeDtypeStruct(queries.shape, BF)
    dma = pltpu.SemaphoreType.DMA
    square = (LM, HD)
    chain = (NST, ITERS, 2) + square
    return pl.pallas_call(
        kernel,
        out_shape=(full, full, full, jax.ShapeDtypeStruct(conv_weight.shape, F32)),
        in_specs=[any_spec] * 4 + [vmem_spec],
        out_specs=(any_spec, any_spec, any_spec, vmem_spec),
        scratch_shapes=[
            pltpu.VMEM((2, 128, 4096), BF),
            pltpu.VMEM((16, 4096), BF),
            pltpu.VMEM((2, 8, 16, 512), BF),
            pltpu.VMEM((2, 4) + square, BF),
            pltpu.VMEM((4, 8, 128), F32),
            pltpu.VMEM((4, 2, RUN, EXT), BF),
            pltpu.VMEM((4, NST, RUNS, RUN, 256), BF),
            pltpu.VMEM((NST, 2, 2, 5, 16, 256), BF),
            pltpu.VMEM((NST, 2, RUNS * RUN, LM), F32),
            pltpu.VMEM((NST, 2, RUNS * RUN, LM), BF),
            pltpu.VMEM((NST, 2, LM, RUNS * RUN), F32),
            pltpu.VMEM((NST, 2, 8, 128), F32),
            pltpu.VMEM((NST, 2, 2) + square, F32),
            pltpu.VMEM((NST, 2) + square, F32),
            pltpu.VMEM((NST, 2, 2) + square, BF),
            pltpu.VMEM((NST, 2, 8, 128), F32),
            pltpu.VMEM((NST,) + square, F32),
            pltpu.VMEM((NST,) + square, F32),
            pltpu.VMEM(chain, BF),
            pltpu.VMEM(chain, BF),
            pltpu.VMEM(chain, BF),
            pltpu.VMEM(chain, BF),
            pltpu.VMEM((NST, 8, 128), F32),
            pltpu.VMEM((NST, 2, 2) + square, BF),
            pltpu.VMEM((NST, 2) + square, BF),
            pltpu.VMEM((2,) + square, F32),
            pltpu.VMEM((NST, 2, 2, 2, LM // 2, HD), BF),
            pltpu.VMEM((2, 2, RUNS * RUN, HD), BF),
            pltpu.VMEM((3, NST, RUNS, RUN, 256), BF),
            pltpu.VMEM((5, 8, 128), F32),
            pltpu.VMEM((9, 8, 128), F32),
            dma((3,)), dma((7,)), dma((7,)), dma, dma,
            dma((NST, 4, 7)), dma((NST, 4, 7)), dma((NST, 4)),
            dma((3,)), dma((3,)), dma((NST,)), dma((NST,)),
            dma((NST, 2)), dma((NST, 2)), dma((NST, 2, 2)), dma((NST, 2, 2)),
            dma((NST,)), dma((NST,)), dma((NST,)), dma((NST,)),
            dma((NST,)), dma((NST,)), dma((NST,)), dma((NST,)),
            dma((NST, 3, 7)), dma((NST, 3, 7)), dma((NST, 3)),
            dma((3,)), dma((3,)), dma((4,)), dma((4,)),
        ],
        compiler_params=pltpu.CompilerParams(
            collective_id=0, has_side_effects=True, vmem_limit_bytes=56 * 2**20
        ),
        cost_estimate=pl.CostEstimate(flops=2 * 10**9, bytes_accessed=7 * 2**20, transcendentals=0),
    )(queries, key_vectors, value_vectors, cotangent, conv_weight)


def solution(mesh):
    return jax.shard_map(
        shards,
        mesh=mesh,
        in_specs=(
            P("dp", "seq", None),
            P("dp", "seq", None),
            P("dp", "seq", None),
            P("dp", "seq", None),
            P("seq", None),
        ),
        out_specs=(
            P("dp", "seq", None),
            P("dp", "seq", None),
            P("dp", "seq", None),
            P("seq", None),
        ),
        check_vma=False,
    )
```

profile of v0, /device:TPU:56, one launch (start us, length us, event | category | flops | bytes accessed | tf_op | source)
XLA Modules:
  0.0 151.6 jit_solution(13915042833098417328)
XLA Ops:
  0.6 145.4 %shard_map.84 = (bf16[1,128,4096]{2,1,0:T(8,128)(2,1)}, bf16[1,128,4096]{2,1,0:T(8,128)(2,1)}, bf16[1,128,4096]{2,1,0:T(8,128)(2,1)}, f32[2,9]{1,0:T(2,128)}) custom-call(bf16[1,128,4096]{2,1,0:T(8,128)(2,1)} %q_in.1, bf16[1,128,4096]{2,1,0:T(8,128)(2,1)} %k_in.1, bf16[1,128,4096]{2,1,0:T(8,128)(2,1)} %v_in.1, bf16[1,128,4096]{2,1,0:T(8,128)(2,1)} %g_in.1, ...), custom_call_target="tpu_custom_call" | custom-call | flops 2000000000 | bytes 7340032 | tf_op jit(solution)/shard_map/pallas_call | solution.py:447
  146.1 0.0 copy-start.1
  146.1 2.4 %copy.13 = bf16[1,128,4096]{2,1,0:T(8,128)(2,1)} copy(bf16[1,128,4096]{2,1,0:T(8,128)(2,1)} %get-tuple-element.8) | data formatting | bytes 2097152
  148.4 0.0 copy-done.1
  148.4 0.0 copy-start
  148.4 1.0 copy.14
  149.4 0.6 copy-done
  150.0 0.0 copy-start.2
  150.0 1.0 copy.15
  151.0 0.0 copy-done.2
  151.0 0.6 copy.16
Async XLA Ops:
  146.1 2.4 %copy-start.1 = (bf16[1,128,4096]{2,1,0:T(8,128)(2,1)S(1)}, bf16[1,128,4096]{2,1,0:T(8,128)(2,1)}, u32[]{:S(2)}) copy-start(bf16[1,128,4096]{2,1,0:T(8,128)(2,1)} %get-tuple-element.9) | copy-start | bytes 3145732
  148.4 1.6 %copy-start = (bf16[1,128,4096]{2,1,0:T(8,128)(2,1)S(1)}, bf16[1,128,4096]{2,1,0:T(8,128)(2,1)}, u32[]{:S(2)}) copy-start(bf16[1,128,4096]{2,1,0:T(8,128)(2,1)} %get-tuple-element.10) | copy-start | bytes 3145732
  150.0 1.0 copy-start.2
where the time goes:
time: 152 us
  Pallas kernels  145 us (95%)
  local copies, waits for them, and re-layouts  5.52 us (4%)
    pallas_call x1, Pallas kernels, shards(): pl.pallas_call(kernel, out_shape=(full, full, full, jax.ShapeDtypeStruct(...  145 us
    unnamed x10, local copies, waits for them, and re-layouts  5.52 us

commit v1 on v0

v1 whole, which is shorter than its diff:
```python
import jax
import jax.numpy as jnp
from jax import lax
from jax.experimental import pallas as pl
from jax.experimental.pallas import tpu as pltpu
from jax.sharding import PartitionSpec as P

HD = 128
LM = 128
ITERS = 6
KW = 9
SEG = 16
SCALE = HD ** (-0.5)
MESH = pl.DeviceIdType.MESH
BF = jnp.bfloat16
F32 = jnp.float32

DP_STEPS = (1, 4, 8)
ROWS = 32
NST = 2
RUNS = 4
RUN = 256
EXT = RUN + 32
ORDER = (1, 0, 3, 2)


def dot(a, b, ca=1, cb=0):
    return lax.dot_general(a, b, (((ca,), (cb,)), ((), ())), preferred_element_type=F32)


def split(x):
    high = x.astype(BF)
    return high, (x - high.astype(F32)).astype(BF)


def mm3(a, b):
    left = jnp.concatenate([a[0], a[1], a[0]], axis=1)
    right = jnp.concatenate([b[0], b[0], b[1]], axis=0)
    return dot(left, right)


def rounded(x):
    return x.astype(BF).astype(F32)


def kernel(
    q_in, k_in, v_in, g_in, w_in,
    dq_out, dk_out, dv_out, lg_in, dw_out,
    qk_full, lm_local, lm_all, marks, w_all, taps_mat,
    land, halo, pack, pack_in, rf, rt, lf, stats, part, part_bf, part_in,
    m_save, inv_save, xt_save, p_save, p2_save, j_save, al_save,
    dkq, dkq_in, mid_grad, lg_out, out_buf, dw_buf, dw_dp,
    s_loc, s_lm, r_lm, s_lmf, r_lmf, s_in, r_in, s_own, s_w, r_w, s_ms, r_ms,
    s_part, r_part, s_halo, r_halo, s_dkq, r_dkq, s_tg, r_tg,
    s_out, r_out, s_outl, s_lgl, s_dw, r_dw, s_dp, r_dp,
):
    dp = lax.axis_index("dp")
    seq = lax.axis_index("seq")
    x = seq // 4
    z = seq % 4
    za = z // 2
    zb = z % 2
    other = 1 - za
    group = x * 2 + zb
    ins = (q_in, k_in, v_in, g_in)
    outs = (dq_out, dk_out, dv_out)
    pending = []

    def member(i):
        p = (group + i) % 8
        return p, (p // 2) * 4 + za * 2 + p % 2

    partner = x * 4 + other * 2 + zb
    cross = x * 4 + other * 2 + (1 - zb)

    def dp_peer(step):
        return dp + step - 2 * step * ((dp // step) % 2)

    def remote(src, dst, ss, rs, to, at=None):
        copy = pltpu.make_async_remote_copy(
            src_ref=src, dst_ref=dst, send_sem=ss, recv_sem=rs,
            device_id=(dp if at is None else at, to), device_id_type=MESH,
        )
        copy.start()
        pending.append(copy)
        return copy

    local = []
    for n, ref in enumerate((q_in, k_in)):
        copy = pltpu.make_async_copy(ref.at[0], qk_full.at[n], s_loc.at[n])
        copy.start()
        local.append(copy)
    w_all[...] = jnp.zeros_like(w_all)
    w_all[z, 0:2, 0:KW] = w_in[...]
    barrier = pltpu.get_barrier_semaphore()
    for i in range(1, 8):
        pl.semaphore_signal(barrier, inc=1, device_id=(dp, member(i)[1]), device_id_type=MESH)
    flip = x * 4 + za * 2 + 1 - zb
    along_z = [(dp, to) for to in (flip, partner, cross)]
    along_z += [(dp_peer(2), to) for to in (seq, flip, partner, cross)]
    for to in along_z[1:]:
        pl.semaphore_signal(barrier, inc=1, device_id=to, device_id_type=MESH)
    for step in DP_STEPS:
        pl.semaphore_signal(barrier, inc=1, device_id=(dp_peer(step), seq), device_id_type=MESH)
    for copy in local:
        copy.wait()
    rows = lax.broadcasted_iota(jnp.int32, (8, 128), 0)
    cols = lax.broadcasted_iota(jnp.int32, (8, 128), 1)
    averager = jnp.where(cols // SEG == rows, 1.0 / SEG, 0.0).astype(BF)
    for c in range(8):
        cut = slice(512 * c, 512 * c + 512)
        lm_local[:, cut] = jnp.concatenate(
            [dot(averager, qk_full[0, :, cut]), dot(averager, qk_full[1, :, cut])], axis=0
        ).astype(BF)
    pl.semaphore_wait(barrier, 16)

    my_cols = pl.ds(pl.multiple_of(group * 512, 512), 512)
    lm_copies = []
    for i in range(1, 8):
        p, to = member(i)
        lm_copies.append(remote(
            lm_local.at[:, pl.ds(pl.multiple_of(p * 512, 512), 512)], lm_all.at[za, group],
            s_lm.at[i - 1], r_lm.at[i - 1], to))
    lm_own = pltpu.make_async_copy(lm_local.at[:, my_cols], lm_all.at[za, group], s_loc.at[2])
    lm_own.start()
    w_copies = [
        remote(w_all.at[z], w_all.at[z], s_w.at[n], r_w.at[n], to)
        for n, to in enumerate((x * 4 + za * 2 + 1 - zb, partner, cross))
    ]
    in_copies = {}

    def issue(st, a):
        if st >= NST:
            return
        got = []
        spot = land.at[a, st, x, pl.ds(pl.multiple_of(zb * 128, 128), 128)]
        for i in range(1, 8):
            p, to = member(i)
            cut = pl.ds(pl.multiple_of(p * 512 + st * 256, 256), 256)
            got.append(remote(
                ins[a].at[0, :, cut], spot, s_in.at[st, a, i - 1], r_in.at[st, a, i - 1], to))
        cut = pl.ds(pl.multiple_of(group * 512 + st * 256, 256), 256)
        own = pltpu.make_async_copy(ins[a].at[0, :, cut], spot, s_own.at[st, a])
        own.start()
        in_copies[st, a] = (got, own)

    issue(0, 1)
    issue(0, 0)

    def arrive(st, a):
        got, own = in_copies[st, a]
        for copy in got:
            copy.wait_recv()
        own.wait()

    for copy in lm_copies:
        copy.wait_recv()
    lm_own.wait()
    lmf = remote(lm_all.at[za], lm_all.at[za], s_lmf, r_lmf, partner)
    issue(0, 3)
    issue(0, 2)
    for copy in w_copies:
        copy.wait_recv()

    t_at = lax.broadcasted_iota(jnp.int32, (RUN, EXT), 0)
    u_at = lax.broadcasted_iota(jnp.int32, (RUN, EXT), 1)
    for h in range(4):
        taps = w_all[2 * zb + h // 2, h % 2 : h % 2 + 1, :]
        band = jnp.zeros((RUN, EXT), F32)
        for j in range(KW):
            band = jnp.where(t_at + 20 - u_at == j, taps[:, j : j + 1], band)
        high, low = split(band)
        taps_mat[h, 0] = high
        taps_mat[h, 1] = low

    lmf.wait_recv()
    lm_values = lm_all[...].astype(F32)
    for h in range(4):
        piece = lm_values[:, :, :, 128 * h : 128 * h + 128]
        marks[0, h] = piece[:, :, 0:8].reshape(LM, HD).astype(BF)
        marks[1, h] = piece[:, :, 8:16].reshape(LM, HD).astype(BF)

    r_at = lax.broadcasted_iota(jnp.int32, (LM, LM), 0)
    c_at = lax.broadcasted_iota(jnp.int32, (LM, LM), 1)
    eye = jnp.where(r_at == c_at, 1.0, 0.0).astype(F32)

    def invert(st):
        state = []
        for h in (2 * st, 2 * st + 1):
            logits = dot(marks[0, h], marks[1, h], 1, 1) * SCALE
            e = jnp.exp(logits - jnp.max(logits, axis=1, keepdims=True))
            middle = e / jnp.sum(e, axis=1, keepdims=True)
            top = jnp.max(jnp.sum(middle, axis=0, keepdims=True), axis=1, keepdims=True)
            side = jnp.max(jnp.sum(middle, axis=1, keepdims=True), axis=0, keepdims=True)
            al = 1.0 / (top * side)
            m_save[h] = middle
            al_save[h] = jnp.broadcast_to(al, (8, 128))
            x0 = al * middle.T
            state.append([x0, mm3(split(middle), split(x0))])
        for it in range(ITERS):
            for j in range(2):
                inv, prod = state[j]
                h = 2 * st + j
                ps = split(prod)
                prod2 = mm3(ps, ps)
                p2s = split(prod2)
                j_mat = 13.0 * eye - 15.0 * prod + mm3(p2s, split(7.0 * eye - prod))
                js = split(j_mat)
                xts = split(inv.T)
                for n in range(2):
                    xt_save[h, it, n] = xts[n]
                    p_save[h, it, n] = ps[n]
                    p2_save[h, it, n] = p2s[n]
                    j_save[h, it, n] = js[n]
                new = 0.25 * mm3(split(inv), js)
                if it < ITERS - 1:
                    prod = 0.25 * (13.0 * prod - 15.0 * prod2 + mm3(p2s, split(7.0 * prod - prod2)))
                state[j] = [new, prod]
        for j in range(2):
            inv_save[2 * st + j] = state[j][0]

    dw_state = {}

    def dw_start():
        place = (dp // 2) % 2 * 4 + z
        dw_buf[place] = dw_buf[8]
        dw_state["z"] = [
            remote(dw_buf.at[8], dw_buf.at[place], s_dw.at[n], r_dw.at[n], to, at=at)
            for n, (at, to) in enumerate(along_z)
        ]

    def dw_step(b):
        if b == 0:
            for copy in dw_state["z"]:
                copy.wait_recv()
            first = dw_buf[z // 2] + dw_buf[z // 2 + 2]
            both = first + (dw_buf[z // 2 + 4] + dw_buf[z // 2 + 6])
            dw_dp[0] = jnp.where(z % 2 == 0, both, jnp.concatenate([both[2:8], both[0:2]], axis=0))
        else:
            dw_state["dp"].wait_recv()
            dw_dp[2 * b] = dw_dp[2 * b - 2] + dw_dp[2 * b - 1]
        if b < 3:
            dw_state["dp"] = remote(
                dw_dp.at[2 * b], dw_dp.at[2 * b + 1], s_dp.at[b], r_dp.at[b], seq,
                at=dp_peer(DP_STEPS[b]))
        else:
            dw_out[...] = dw_dp[6]

    at64, at16 = (lax.broadcasted_iota(jnp.int32, (16, n), 1) for n in (64, 16))
    to64, to16 = (lax.broadcasted_iota(jnp.int32, (16, n), 0) for n in (64, 16))

    def ones_where(cond):
        return jnp.where(cond, 1.0, 0.0).astype(BF)

    pick_first = ones_where(at64 == (to64 // 4) * 16 + to64 % 4)
    pick_final = ones_where(at64 == (to64 // 4) * 16 + 12 + to64 % 4)
    spread = (
        [ones_where((at16 // 4 == r - 1 + za) & (to16 == 12 + at16 % 4)) for r in range(RUNS)],
        [ones_where((at16 // 4 == r + za) & (to16 == at16 % 4)) for r in range(RUNS)],
    )
    dw_buf[8] = jnp.zeros((8, 128), F32)
    lane = lax.broadcasted_iota(jnp.int32, (1, 128), 1)

    out_copies = {(st, a): [] for st in range(NST) for a in range(3)}
    own_out = {}
    lg_copies = {}

    def finish(st):
        for copy in lg_copies[st]:
            copy.wait_recv()
        for a in (2, 1, 0):
            for copy in out_copies[st, a]:
                copy.wait_recv()
            own_out[st, a].wait()
        own_out[st, 3].wait()

    def head(st, a, j):
        return land[a, st, :, :, 128 * j : 128 * j + 128].reshape(RUNS * RUN, HD)

    def send_halo(st):
        first = land[3, st, :, 0:16, :].reshape(RUNS * 16, 256)
        final = land[3, st, :, RUN - 16 : RUN, :].reshape(RUNS * 16, 256)
        pack[st, 0] = dot(pick_final, final).astype(BF)
        pack[st, 1] = dot(pick_first, first).astype(BF)
        return remote(pack.at[st], pack_in.at[st], s_halo.at[st], r_halo.at[st], partner)

    def extended(st, r, j):
        cut = slice(128 * j, 128 * j + 128)
        return jnp.concatenate(
            [halo[st, 0, r, :, cut], land[3, st, r, :, cut], halo[st, 1, r, :, cut]], axis=0)

    sent = {}

    def prepare(st):
        arrive(st, 1)
        for j in range(2):
            logits = dot(head(st, 1, j), marks[0, 2 * st + j], 1, 1) * SCALE
            m = jnp.max(logits, axis=0, keepdims=True)
            e = jnp.exp(logits - m)
            rf[st, j] = e
            stats[st, za, 2 * j : 2 * j + 1, :] = m
            stats[st, za, 2 * j + 1 : 2 * j + 2, :] = jnp.sum(e, axis=0, keepdims=True)
        ms = remote(stats.at[st, za], stats.at[st, za], s_ms.at[st], r_ms.at[st], partner)
        if st == 0:
            for a in ORDER:
                issue(1, a)
        arrive(st, 0)
        for j in range(2):
            logits = dot(marks[1, 2 * st + j], head(st, 0, j), 1, 1) * SCALE
            e = jnp.exp(logits - jnp.max(logits, axis=0, keepdims=True))
            lf[st, j] = e * (1.0 / jnp.sum(e, axis=0, keepdims=True))
        invert(st)
        arrive(st, 3)
        for j in range(2):
            part[st, 0, j] = dot(lf[st, j].astype(BF), head(st, 3, j))
            part_bf[st, 0, j] = part[st, 0, j].astype(BF)
        sent[st, "dm"] = remote(
            part_bf.at[st, 0], part_in.at[st, 0], s_part.at[st, 0], r_part.at[st, 0], partner)
        sent[st, "halo"] = send_halo(st)
        ms.wait_recv()
        for j in range(2):
            m1 = stats[st, za, 2 * j : 2 * j + 1, :]
            s1 = stats[st, za, 2 * j + 1 : 2 * j + 2, :]
            m2 = stats[st, other, 2 * j : 2 * j + 1, :]
            s2 = stats[st, other, 2 * j + 1 : 2 * j + 2, :]
            m = jnp.maximum(m1, m2)
            e1 = jnp.exp(m1 - m)
            factor = e1 / (s1 * e1 + s2 * jnp.exp(m2 - m))
            value = rf[st, j] * factor
            rf[st, j] = value
            rt[st, j] = value.astype(BF)
        arrive(st, 2)
        for j in range(2):
            part[st, 1, j] = dot(rt[st, j], head(st, 2, j), 0, 0)
            part_bf[st, 1, j] = part[st, 1, j].astype(BF)
        sent[st, "sum"] = remote(
            part_bf.at[st, 1], part_in.at[st, 1], s_part.at[st, 1], r_part.at[st, 1], partner)

    def convolve(st):
        sent[st, "halo"].wait_recv()
        for side in range(2):
            packed = pack_in[st, side]
            for r in range(RUNS):
                halo[st, side, r] = dot(spread[side][r], packed).astype(BF)
        for j in range(2):
            for r in range(RUNS):
                g_ext = extended(st, r, j)
                conv = dot(taps_mat[2 * st + j, 0], g_ext) + dot(taps_mat[2 * st + j, 1], g_ext)
                out_buf[2, st, r, :, 128 * j : 128 * j + 128] = conv.astype(BF)

    def taps_grad(st):
        for j in range(2):
            corr = jnp.zeros((RUN, EXT), F32)
            for r in range(RUNS):
                cut = slice(128 * j, 128 * j + 128)
                corr += dot(land[2, st, r, :, cut], extended(st, r, j), 1, 1)
            line = jnp.zeros((1, 128), F32)
            for t in range(KW):
                band = jnp.where(t_at + 20 - u_at == t, corr, 0.0)
                total = jnp.sum(jnp.sum(band, axis=0, keepdims=True), axis=1, keepdims=True)
                line = jnp.where(lane == t, total, line)
            dw_buf[8, 2 * st + j : 2 * st + j + 1, :] = line

    def totals(st, j):
        dms = (part[st, 0, j] + part_in[st, 0, j].astype(F32)).astype(BF)
        return dms, part[st, 1, j] + part_in[st, 1, j].astype(F32)

    def send_out(st, a):
        spot = outs[a].at[0, :, pl.ds(pl.multiple_of(group * 512 + st * 256, 256), 256)]
        for i in range(1, 8):
            p, to = member(i)
            out_copies[st, a].append(remote(
                out_buf.at[a, st, p // 2, pl.ds(pl.multiple_of((p % 2) * 128, 128), 128)], spot,
                s_out.at[st, a, i - 1], r_out.at[st, a, i - 1], to))
        copy = pltpu.make_async_copy(
            out_buf.at[a, st, x, pl.ds(pl.multiple_of(zb * 128, 128), 128)], spot,
            s_outl.at[st, a])
        copy.start()
        own_out[st, a] = copy

    def grads(st):
        sent[st, "dm"].wait_recv()
        sent[st, "sum"].wait_recv()
        mixeds, dsums, deltas = [], [], []
        for j in range(2):
            dms, summary = totals(st, j)
            inv = inv_save[2 * st + j]
            inv_t = split(inv.T)
            mixed = jnp.dot(
                inv, summary, precision=lax.Precision.HIGHEST, preferred_element_type=F32)
            dsum = dot(jnp.concatenate([inv_t[0], inv_t[1]], axis=1),
                       jnp.concatenate([dms, dms], axis=0))
            mixeds.append(mixed.astype(BF))
            dsums.append(dsum.astype(BF))
            deltas.append(jnp.sum((dsum * summary).T, axis=0, keepdims=True))
        for j in range(2):
            cut = slice(128 * j, 128 * j + 128)
            d_v = rounded(dot(rt[st, j], dsums[j])).reshape(RUNS, RUN, HD)
            out_buf[2, st, :, :, cut] = (out_buf[2, st, :, :, cut].astype(F32) + d_v).astype(BF)
        send_out(st, 2)
        for j in range(2):
            cut = slice(128 * j, 128 * j + 128)
            d_right = rounded(dot(head(st, 2, j), dsums[j], 1, 1))
            d_right = (rf[st, j] * (d_right - deltas[j]) * SCALE).astype(BF)
            d_k = dot(d_right, marks[0, 2 * st + j]).astype(BF)
            out_buf[1, st, :, :, cut] = d_k.reshape(RUNS, RUN, HD)
            dkq[st, 0, :, j] = dot(d_right, head(st, 1, j), 0, 0).astype(BF).reshape(
                2, LM // 2, HD)
        for j in range(2):
            cut = slice(128 * j, 128 * j + 128)
            left = lf[st, j]
            d_left = rounded(dot(mixeds[j], head(st, 3, j), 1, 1))
            prod = left * d_left
            d_left = ((prod - left * jnp.sum(prod, axis=0, keepdims=True)) * SCALE).astype(BF)
            d_q = dot(d_left, marks[1, 2 * st + j], 0, 0).astype(BF)
            out_buf[0, st, :, :, cut] = d_q.reshape(RUNS, RUN, HD)
            dkq[st, 1, :, j] = dot(d_left, head(st, 0, j)).astype(BF).reshape(2, LM // 2, HD)
        sent[st, "dkq"] = remote(
            dkq.at[st, :, other], dkq_in.at[st], s_dkq.at[st], r_dkq.at[st], partner)

    def reverse(st):
        chain = []
        for j in range(2):
            dms, summary = totals(st, j)
            s_t = split(summary.T)
            grad = dot(
                jnp.concatenate([dms, dms], axis=1), jnp.concatenate([s_t[0], s_t[1]], axis=0))
            chain.append([grad, jnp.zeros((LM, LM), F32), split(m_save[2 * st + j].T)])
        for it in reversed(range(ITERS)):
            for j in range(2):
                h = 2 * st + j
                grad, d_mid, m_t = chain[j]
                xt = (xt_save[h, it, 0], xt_save[h, it, 1])
                ps = (p_save[h, it, 0], p_save[h, it, 1])
                p2s = (p2_save[h, it, 0], p2_save[h, it, 1])
                js = (j_save[h, it, 0], j_save[h, it, 1])
                ws = split(grad)
                g_mat = 0.25 * mm3(xt, ws)
                gs = split(g_mat)
                u_mat = 7.0 * g_mat - mm3(gs, ps)
                us = split(u_mat)
                d_p = mm3(us, ps) + mm3(ps, us) - mm3(p2s, gs) - 15.0 * g_mat
                dps = split(d_p)
                d_mid = d_mid + mm3(dps, xt)
                grad = 0.25 * mm3(ws, js) + mm3(m_t, dps)
                chain[j] = [grad, d_mid, m_t]
        for j in range(2):
            h = 2 * st + j
            grad, d_mid, m_t = chain[j]
            middle = m_save[h]
            d_mid = d_mid + al_save[h, 0:1, :] * grad.T
            d_log = middle * (d_mid - jnp.sum(middle * d_mid, axis=1, keepdims=True)) * SCALE
            d_log = d_log.astype(BF)
            mid_grad[0, j] = dot(d_log, marks[1, h]).reshape(2, LM // 2, HD)
            mid_grad[1, j] = dot(d_log, marks[0, h], 0, 0).reshape(2, LM // 2, HD)
        sent[st, "dkq"].wait_recv()
        for j in range(2):
            cut = slice(128 * j, 128 * j + 128)
            both = []
            for n in range(2):
                rest = rounded(dkq[st, n, za, j].astype(F32) + dkq_in[st, n, j].astype(F32))
                rest = rounded(rest + rounded(mid_grad[n, j, za])) * (1.0 / SEG)
                both.append(rest.reshape(8, 8, HD))
            lg_out[st, :, :, cut] = jnp.concatenate(both, axis=1).astype(BF)
        lg_copies[st] = []
        spot = pl.ds(pl.multiple_of(group * 512 + st * 256, 256), 256)
        for i in range(1, 8):
            p, to = member(i)
            lg_copies[st].append(remote(
                lg_out.at[st, p], lg_in.at[:, spot], s_tg.at[st, i - 1], r_tg.at[st, i - 1], to))
        own = pltpu.make_async_copy(lg_out.at[st, group], lg_in.at[:, spot], s_lgl.at[st])
        own.start()
        own_out[st, 3] = own

    prepare(0)
    prepare(1)
    convolve(0)
    grads(0)
    convolve(1)
    taps_grad(0)
    taps_grad(1)
    dw_start()
    grads(1)
    for st in range(NST):
        send_out(st, 1)
        send_out(st, 0)
    dw_step(0)
    reverse(0)
    dw_step(1)
    reverse(1)
    dw_step(2)
    for st in range(NST):
        finish(st)
    dw_step(3)
    for copy in pending:
        copy.wait_send()


def add_marks(dq, dk, dv, marks_grad, dw, dq_out, dk_out, dv_out, dw_out):
    at = (pl.program_id(0) * ROWS + lax.broadcasted_iota(jnp.int32, (ROWS, 16), 0)) // SEG
    col = lax.broadcasted_iota(jnp.int32, (ROWS, 16), 1)
    for n, (part, out) in enumerate(((dq, dq_out), (dk, dk_out))):
        pick = jnp.where(col == at + 8 * n, 1.0, 0.0).astype(BF)
        out[0] = (part[0].astype(F32) + dot(pick, marks_grad[...])).astype(BF)
    dv_out[...] = dv[...]
    dw_out[...] = dw[0:2, 0:KW]


def shards(queries, key_vectors, value_vectors, cotangent, conv_weight):
    any_spec = pl.BlockSpec(memory_space=pl.ANY)
    vmem_spec = pl.BlockSpec(memory_space=pltpu.VMEM)
    full = jax.ShapeDtypeStruct(queries.shape, BF)
    dma = pltpu.SemaphoreType.DMA
    square = (LM, HD)
    chain = (4, ITERS, 2) + square
    dq, dk, dv, marks_grad, dw = pl.pallas_call(
        kernel,
        out_shape=(
            full, full, full, jax.ShapeDtypeStruct((16, full.shape[2]), BF),
            jax.ShapeDtypeStruct((8, 128), F32)),
        in_specs=[any_spec] * 4 + [vmem_spec],
        out_specs=(any_spec,) * 4 + (vmem_spec,),
        scratch_shapes=[
            pltpu.VMEM((2, 128, 4096), BF),
            pltpu.VMEM((16, 4096), BF),
            pltpu.VMEM((2, 8, 16, 512), BF),
            pltpu.VMEM((2, 4) + square, BF),
            pltpu.VMEM((4, 8, 128), F32),
            pltpu.VMEM((4, 2, RUN, EXT), BF),
            pltpu.VMEM((4, NST, RUNS, RUN, 256), BF),
            pltpu.VMEM((NST, 2, RUNS, 16, 256), BF),
            pltpu.VMEM((NST, 2, 16, 256), BF),
            pltpu.VMEM((NST, 2, 16, 256), BF),
            pltpu.VMEM((NST, 2, RUNS * RUN, LM), F32),
            pltpu.VMEM((NST, 2, RUNS * RUN, LM), BF),
            pltpu.VMEM((NST, 2, LM, RUNS * RUN), F32),
            pltpu.VMEM((NST, 2, 8, 128), F32),
            pltpu.VMEM((NST, 2, 2) + square, F32),
            pltpu.VMEM((NST, 2, 2) + square, BF),
            pltpu.VMEM((NST, 2, 2) + square, BF),
            pltpu.VMEM((4,) + square, F32),
            pltpu.VMEM((4,) + square, F32),
            pltpu.VMEM(chain, BF),
            pltpu.VMEM(chain, BF),
            pltpu.VMEM(chain, BF),
            pltpu.VMEM(chain, BF),
            pltpu.VMEM((4, 8, 128), F32),
            pltpu.VMEM((NST, 2, 2, 2, LM // 2, HD), BF),
            pltpu.VMEM((NST, 2, 2, LM // 2, HD), BF),
            pltpu.VMEM((2, 2, 2, LM // 2, HD), F32),
            pltpu.VMEM((NST, 8, 16, 256), BF),
            pltpu.VMEM((3, NST, RUNS, RUN, 256), BF),
            pltpu.VMEM((9, 8, 128), F32),
            pltpu.VMEM((7, 8, 128), F32),
            dma((3,)), dma((7,)), dma((7,)), dma, dma,
            dma((NST, 4, 7)), dma((NST, 4, 7)), dma((NST, 4)),
            dma((3,)), dma((3,)), dma((NST,)), dma((NST,)),
            dma((NST, 2)), dma((NST, 2)), dma((NST,)), dma((NST,)),
            dma((NST,)), dma((NST,)), dma((NST, 7)), dma((NST, 7)),
            dma((NST, 3, 7)), dma((NST, 3, 7)), dma((NST, 3)), dma((NST,)),
            dma((7,)), dma((7,)), dma((3,)), dma((3,)),
        ],
        compiler_params=pltpu.CompilerParams(
            collective_id=0, has_side_effects=True, vmem_limit_bytes=56 * 2**20
        ),
        cost_estimate=pl.CostEstimate(flops=2 * 10**9, bytes_accessed=7 * 2**20, transcendentals=0),
    )(queries, key_vectors, value_vectors, cotangent, conv_weight)
    block = pl.BlockSpec((1, ROWS, full.shape[2]), lambda i: (0, i, 0))

    def whole(shape):
        return pl.BlockSpec(shape, lambda i: (0, 0))

    return pl.pallas_call(
        add_marks,
        grid=(full.shape[1] // ROWS,),
        out_shape=(full, full, full, jax.ShapeDtypeStruct(conv_weight.shape, F32)),
        in_specs=[block] * 3 + [whole(marks_grad.shape), whole(dw.shape)],
        out_specs=(block, block, block, whole(conv_weight.shape)),
        compiler_params=pltpu.CompilerParams(vmem_limit_bytes=60 * 2**20),
    )(dq, dk, dv, marks_grad, dw)


def solution(mesh):
    return jax.shard_map(
        shards,
        mesh=mesh,
        in_specs=(
            P("dp", "seq", None),
            P("dp", "seq", None),
            P("dp", "seq", None),
            P("dp", "seq", None),
            P("seq", None),
        ),
        out_specs=(
            P("dp", "seq", None),
            P("dp", "seq", None),
            P("dp", "seq", None),
            P("seq", None),
        ),
        check_vma=False,
    )
```

time: 152 us -> 116 us (0.76)
  Pallas kernels: 145 us -> 116 us
  local copies, waits for them, and re-layouts: 5.52 us -> 0 us
    pallas_call x1, Pallas kernels: 145 us -> 111 us  [shards(): pl.pallas_call(kernel, out_shape=(full, full, full, jax.ShapeDtypeStruct(...]
    unnamed x10 -> x0, local copies, waits for them, and re-layouts: 5.52 us -> none
    pallas_call x0 -> x1, Pallas kernels: none -> 4.58 us  [shards(): pl.pallas_call(add_marks, grid=(full.shape[1] // ROWS,), out_shape=(full,...]
where the time goes in v1:
time: 116 us
  Pallas kernels  116 us (100%)
    pallas_call x1, Pallas kernels, shards(): pl.pallas_call(kernel, out_shape=(full, full, full, jax.ShapeDtypeStruct(...  111 us
    pallas_call x1, Pallas kernels, shards(): pl.pallas_call(add_marks, grid=(full.shape[1] // ROWS,), out_shape=(full,...  4.58 us

profile of v1, /device:TPU:56, one launch (start us, length us, event | category | flops | bytes accessed | tf_op | source)
XLA Modules:
  0.0 116.2 jit_solution(948316232859934146)
XLA Ops:
  0.6 111.0 %shard_map.84 = (bf16[1,128,4096]{2,1,0:T(8,128)(2,1)}, bf16[1,128,4096]{2,1,0:T(8,128)(2,1)}, bf16[1,128,4096]{2,1,0:T(8,128)(2,1)}, bf16[16,4096]{1,0:T(8,128)(2,1)}, f32[8,128]{1,0:T(8,128)}) custom-call(bf16[1,128,4096]{2,1,0:T(8,128)(2,1)} %q_in.1, bf16[1,128,4096]{2,1,0:T(8,128)(2,1)} %k_in.1, bf16[1,128,4096]{2,1,0:T(8,128)(2,1)} %v_in.1, ...), custom_call_target="tpu_custom_call" | custom-call | flops 2000000000 | bytes 7340032 | tf_op jit(solution)/shard_map/pallas_call | solution.py:516
  111.6 4.6 %shard_map.85 = (bf16[1,128,4096]{2,1,0:T(8,128)(2,1)}, bf16[1,128,4096]{2,1,0:T(8,128)(2,1)}, bf16[1,128,4096]{2,1,0:T(8,128)(2,1)}, f32[2,9]{1,0:T(2,128)}) custom-call(bf16[1,128,4096]{2,1,0:T(8,128)(2,1)} %get-tuple-element.9.dq, bf16[1,128,4096]{2,1,0:T(8,128)(2,1)} %get-tuple-element.10.dk, bf16[1,128,4096]{2,1,0:T(8,128)(2,1)} %get-tuple-element.11.dv, ...), custom_call_target="tpu_custom_call" | custom-call | tf_op jit(solution)/shard_map/pallas_call | solution.py:573

commit v2 on v1

--- a/solution.py
+++ b/solution.py
@@ -16,7 +16,7 @@
 F32 = jnp.float32
 
 DP_STEPS = (1, 4, 8)
-ROWS = 32
+ROWS = 64
 NST = 2
 RUNS = 4
 RUN = 256
@@ -102,31 +102,7 @@
         pl.semaphore_signal(barrier, inc=1, device_id=to, device_id_type=MESH)
     for step in DP_STEPS:
         pl.semaphore_signal(barrier, inc=1, device_id=(dp_peer(step), seq), device_id_type=MESH)
-    for copy in local:
-        copy.wait()
-    rows = lax.broadcasted_iota(jnp.int32, (8, 128), 0)
-    cols = lax.broadcasted_iota(jnp.int32, (8, 128), 1)
-    averager = jnp.where(cols // SEG == rows, 1.0 / SEG, 0.0).astype(BF)
-    for c in range(8):
-        cut = slice(512 * c, 512 * c + 512)
-        lm_local[:, cut] = jnp.concatenate(
-            [dot(averager, qk_full[0, :, cut]), dot(averager, qk_full[1, :, cut])], axis=0
-        ).astype(BF)
     pl.semaphore_wait(barrier, 16)
-
-    my_cols = pl.ds(pl.multiple_of(group * 512, 512), 512)
-    lm_copies = []
-    for i in range(1, 8):
-        p, to = member(i)
-        lm_copies.append(remote(
-            lm_local.at[:, pl.ds(pl.multiple_of(p * 512, 512), 512)], lm_all.at[za, group],
-            s_lm.at[i - 1], r_lm.at[i - 1], to))
-    lm_own = pltpu.make_async_copy(lm_local.at[:, my_cols], lm_all.at[za, group], s_loc.at[2])
-    lm_own.start()
-    w_copies = [
-        remote(w_all.at[z], w_all.at[z], s_w.at[n], r_w.at[n], to)
-        for n, to in enumerate((x * 4 + za * 2 + 1 - zb, partner, cross))
-    ]
     in_copies = {}
 
     def issue(st, a):
@@ -145,6 +121,30 @@
         in_copies[st, a] = (got, own)
 
     issue(0, 1)
+    for copy in local:
+        copy.wait()
+    rows = lax.broadcasted_iota(jnp.int32, (8, 128), 0)
+    cols = lax.broadcasted_iota(jnp.int32, (8, 128), 1)
+    averager = jnp.where(cols // SEG == rows, 1.0 / SEG, 0.0).astype(BF)
+    for c in range(8):
+        cut = slice(512 * c, 512 * c + 512)
+        lm_local[:, cut] = jnp.concatenate(
+            [dot(averager, qk_full[0, :, cut]), dot(averager, qk_full[1, :, cut])], axis=0
+        ).astype(BF)
+
+    my_cols = pl.ds(pl.multiple_of(group * 512, 512), 512)
+    lm_copies = []
+    for i in range(1, 8):
+        p, to = member(i)
+        lm_copies.append(remote(
+            lm_local.at[:, pl.ds(pl.multiple_of(p * 512, 512), 512)], lm_all.at[za, group],
+            s_lm.at[i - 1], r_lm.at[i - 1], to))
+    lm_own = pltpu.make_async_copy(lm_local.at[:, my_cols], lm_all.at[za, group], s_loc.at[2])
+    lm_own.start()
+    w_copies = [
+        remote(w_all.at[z], w_all.at[z], s_w.at[n], r_w.at[n], to)
+        for n, to in enumerate((x * 4 + za * 2 + 1 - zb, partner, cross))
+    ]
     issue(0, 0)
 
     def arrive(st, a):
@@ -302,8 +302,8 @@
             stats[st, za, 2 * j + 1 : 2 * j + 2, :] = jnp.sum(e, axis=0, keepdims=True)
         ms = remote(stats.at[st, za], stats.at[st, za], s_ms.at[st], r_ms.at[st], partner)
         if st == 0:
-            for a in ORDER:
-                issue(1, a)
+            issue(1, 1)
+            issue(1, 0)
         arrive(st, 0)
         for j in range(2):
             logits = dot(marks[1, 2 * st + j], head(st, 0, j), 1, 1) * SCALE
@@ -317,7 +317,10 @@
         sent[st, "dm"] = remote(
             part_bf.at[st, 0], part_in.at[st, 0], s_part.at[st, 0], r_part.at[st, 0], partner)
         sent[st, "halo"] = send_halo(st)
-        ms.wait_recv()
+        sent[st, "ms"] = ms
+
+    def sum_up(st):
+        sent[st, "ms"].wait_recv()
         for j in range(2):
             m1 = stats[st, za, 2 * j : 2 * j + 1, :]
             s1 = stats[st, za, 2 * j + 1 : 2 * j + 2, :]
@@ -451,15 +454,17 @@
             d_mid = d_mid + al_save[h, 0:1, :] * grad.T
             d_log = middle * (d_mid - jnp.sum(middle * d_mid, axis=1, keepdims=True)) * SCALE
             d_log = d_log.astype(BF)
-            mid_grad[0, j] = dot(d_log, marks[1, h]).reshape(2, LM // 2, HD)
-            mid_grad[1, j] = dot(d_log, marks[0, h], 0, 0).reshape(2, LM // 2, HD)
+            mid_grad[st, 0, j] = dot(d_log, marks[1, h]).reshape(2, LM // 2, HD)
+            mid_grad[st, 1, j] = dot(d_log, marks[0, h], 0, 0).reshape(2, LM // 2, HD)
+
+    def send_marks(st):
         sent[st, "dkq"].wait_recv()
         for j in range(2):
             cut = slice(128 * j, 128 * j + 128)
             both = []
             for n in range(2):
                 rest = rounded(dkq[st, n, za, j].astype(F32) + dkq_in[st, n, j].astype(F32))
-                rest = rounded(rest + rounded(mid_grad[n, j, za])) * (1.0 / SEG)
+                rest = rounded(rest + rounded(mid_grad[st, n, j, za])) * (1.0 / SEG)
                 both.append(rest.reshape(8, 8, HD))
             lg_out[st, :, :, cut] = jnp.concatenate(both, axis=1).astype(BF)
         lg_copies[st] = []
@@ -473,21 +478,28 @@
         own_out[st, 3] = own
 
     prepare(0)
+    sum_up(0)
+    issue(1, 3)
+    issue(1, 2)
     prepare(1)
     convolve(0)
     grads(0)
+    sum_up(1)
     convolve(1)
     taps_grad(0)
     taps_grad(1)
     dw_start()
+    send_out(0, 1)
+    send_out(0, 0)
+    reverse(0)
     grads(1)
-    for st in range(NST):
-        send_out(st, 1)
-        send_out(st, 0)
+    send_out(1, 1)
+    send_out(1, 0)
+    send_marks(0)
+    reverse(1)
+    send_marks(1)
     dw_step(0)
-    reverse(0)
     dw_step(1)
-    reverse(1)
     dw_step(2)
     for st in range(NST):
         finish(st)
@@ -547,7 +559,7 @@
             pltpu.VMEM((4, 8, 128), F32),
             pltpu.VMEM((NST, 2, 2, 2, LM // 2, HD), BF),
             pltpu.VMEM((NST, 2, 2, LM // 2, HD), BF),
-            pltpu.VMEM((2, 2, 2, LM // 2, HD), F32),
+            pltpu.VMEM((NST, 2, 2, 2, LM // 2, HD), F32),
             pltpu.VMEM((NST, 8, 16, 256), BF),
             pltpu.VMEM((3, NST, RUNS, RUN, 256), BF),
             pltpu.VMEM((9, 8, 128), F32),
@@ -561,7 +573,7 @@
             dma((7,)), dma((7,)), dma((3,)), dma((3,)),
         ],
         compiler_params=pltpu.CompilerParams(
-            collective_id=0, has_side_effects=True, vmem_limit_bytes=56 * 2**20
+            collective_id=0, has_side_effects=True, vmem_limit_bytes=50 * 2**20
         ),
         cost_estimate=pl.CostEstimate(flops=2 * 10**9, bytes_accessed=7 * 2**20, transcendentals=0),
     )(queries, key_vectors, value_vectors, cotangent, conv_weight)
@@ -576,7 +588,7 @@
         out_shape=(full, full, full, jax.ShapeDtypeStruct(conv_weight.shape, F32)),
         in_specs=[block] * 3 + [whole(marks_grad.shape), whole(dw.shape)],
         out_specs=(block, block, block, whole(conv_weight.shape)),
-        compiler_params=pltpu.CompilerParams(vmem_limit_bytes=60 * 2**20),
+        compiler_params=pltpu.CompilerParams(vmem_limit_bytes=30 * 2**20),
     )(dq, dk, dv, marks_grad, dw)
 
 

time: 116 us -> 112 us (0.966)
  Pallas kernels: 116 us -> 110 us
    pallas_call x1, Pallas kernels: 111 us -> 108 us  [shards(): pl.pallas_call(kernel, out_shape=(full, full, full, jax.ShapeDtypeStruct(...]
    pallas_call x1, Pallas kernels: 4.58 us -> 1.97 us  [shards(): pl.pallas_call(add_marks, grid=(full.shape[1] // ROWS,), out_shape=(full,...]
where the time goes in v2:
time: 112 us; the launch traced here: 111 us
  Pallas kernels  110 us (98%)
    pallas_call x1, Pallas kernels, shards(): pl.pallas_call(kernel, out_shape=(full, full, full, jax.ShapeDtypeStruct(...  108 us

profile of v2, /device:TPU:56, one launch (start us, length us, event | category | flops | bytes accessed | tf_op | source)
XLA Modules:
  0.0 111.1 jit_solution(4340876698649529950)
XLA Ops:
  0.6 0.0 copy-start
  0.6 0.7 copy-done
  1.3 107.8 %shard_map.84 = (bf16[1,128,4096]{2,1,0:T(8,128)(2,1)S(1)}, bf16[1,128,4096]{2,1,0:T(8,128)(2,1)S(1)}, bf16[1,128,4096]{2,1,0:T(8,128)(2,1)S(1)}, bf16[16,4096]{1,0:T(8,128)(2,1)S(1)}, f32[8,128]{1,0:T(8,128)S(1)}) custom-call(bf16[1,128,4096]{2,1,0:T(8,128)(2,1)} %q_in.1, bf16[1,128,4096]{2,1,0:T(8,128)(2,1)} %k_in.1, bf16[1,128,4096]{2,1,0:T(8,128)(2,1)} %v_in.1, ...), custom_call_target="tpu_custom_call" | custom-call | flops 2000000000 | bytes 7340032 | tf_op jit(solution)/shard_map/pallas_call | solution.py:528
  109.1 2.0 %shard_map.85 = (bf16[1,128,4096]{2,1,0:T(8,128)(2,1)}, bf16[1,128,4096]{2,1,0:T(8,128)(2,1)}, bf16[1,128,4096]{2,1,0:T(8,128)(2,1)}, f32[2,9]{1,0:T(2,128)}) custom-call(bf16[1,128,4096]{2,1,0:T(8,128)(2,1)S(1)} %get-tuple-element.9.dq, bf16[1,128,4096]{2,1,0:T(8,128)(2,1)S(1)} %get-tuple-element.10.dk, bf16[1,128,4096]{2,1,0:T(8,128)(2,1)S(1)} %get-tuple-element.11.dv, ...), custom_call_target="tpu_custom_call" | custom-call | tf_op jit(solution)/shard_map/pallas_call | solution.py:585
Async XLA Ops:
  0.6 0.7 copy-start

commit v3 on v2

--- a/solution.py
+++ b/solution.py
@@ -16,7 +16,7 @@
 F32 = jnp.float32
 
 DP_STEPS = (1, 4, 8)
-ROWS = 64
+ROWS = 32
 NST = 2
 RUNS = 4
 RUN = 256

time: 112 us -> 113 us (level)
  no operation moved by 1% of the time
where the time goes in v3:
time: 113 us; the launch traced here: 112 us
  Pallas kernels  110 us (97%)
    pallas_call x1, Pallas kernels, shards(): pl.pallas_call(kernel, out_shape=(full, full, full, jax.ShapeDtypeStruct(...  108 us
    pallas_call x1, Pallas kernels, shards(): pl.pallas_call(add_marks, grid=(full.shape[1] // ROWS,), out_shape=(full,...  2.5 us

profile of v3, /device:TPU:56, one launch (start us, length us, event | category | flops | bytes accessed | tf_op | source)
XLA Modules:
  0.0 111.6 jit_solution(13136262728915621448)
XLA Ops:
  0.6 0.0 copy-start
  0.6 0.7 copy-done
  1.3 107.8 %shard_map.84 = (bf16[1,128,4096]{2,1,0:T(8,128)(2,1)S(1)}, bf16[1,128,4096]{2,1,0:T(8,128)(2,1)S(1)}, bf16[1,128,4096]{2,1,0:T(8,128)(2,1)S(1)}, bf16[16,4096]{1,0:T(8,128)(2,1)S(1)}, f32[8,128]{1,0:T(8,128)S(1)}) custom-call(bf16[1,128,4096]{2,1,0:T(8,128)(2,1)} %q_in.1, bf16[1,128,4096]{2,1,0:T(8,128)(2,1)} %k_in.1, bf16[1,128,4096]{2,1,0:T(8,128)(2,1)} %v_in.1, ...), custom_call_target="tpu_custom_call" | custom-call | flops 2000000000 | bytes 7340032 | tf_op jit(solution)/shard_map/pallas_call | solution.py:528
  109.1 2.5 %shard_map.85 = (bf16[1,128,4096]{2,1,0:T(8,128)(2,1)}, bf16[1,128,4096]{2,1,0:T(8,128)(2,1)}, bf16[1,128,4096]{2,1,0:T(8,128)(2,1)}, f32[2,9]{1,0:T(2,128)}) custom-call(bf16[1,128,4096]{2,1,0:T(8,128)(2,1)S(1)} %get-tuple-element.9.dq, bf16[1,128,4096]{2,1,0:T(8,128)(2,1)S(1)} %get-tuple-element.10.dk, bf16[1,128,4096]{2,1,0:T(8,128)(2,1)S(1)} %get-tuple-element.11.dv, ...), custom_call_target="tpu_custom_call" | custom-call | tf_op jit(solution)/shard_map/pallas_call | solution.py:585
Async XLA Ops:
  0.6 0.7 copy-start
